TPU v7x, 32 devices: a whole 2x2x4 slice. The times are simulated.
32 devices in a mesh: group: 2 (over y), ens: 4 (over z), row: 2 (over x), col: 2 (over core).
Axes of the slice: x: 2, y: 2, z: 4, core: 2. Of those that a mesh axis runs over, the one named last changes fastest.
Arguments:
- fields: bfloat16 [4, 128, 256, 128], P('ens', ('group', 'row'), 'col'), parts along dimension 1, may hold values from -6 to 6
- conv_weight: bfloat16 [7, 7, 128], replicated, may hold values from -0.875 to 0.875
- conv_gain: bfloat16 [128], replicated, may hold values from 0.099609375 to 1.8984375
- mlp_in: bfloat16 [128, 512], replicated, may hold values from -0.5 to 0.5
- mlp_out: bfloat16 [512, 128], replicated, may hold values from -0.25 to 0.25
- layer_scale: bfloat16 [128], replicated, may hold values from 0.099609375 to 1.8984375
- attn_gain: bfloat16 [128], replicated, may hold values from 0.099609375 to 1.8984375
- qkv_weight: bfloat16 [3, 128, 128], replicated, may hold values from -1 to 1
- out_weight: bfloat16 [128, 128], replicated, may hold values from -0.5 to 0.5
Outputs:
- result: bfloat16 [4, 128, 256, 128], P('ens', ('group', 'row'), 'col'), parts along dimension 1
There are 2 independent parts, one for each index of `group`. A program takes and returns all parts, laid end to end along the dimension named above; an argument that names none is the same for every part. Nothing has to cross between parts.
All inputs are finite; a program needn't handle non-finite values.
Results may differ from a plain program's by a relative error of at most 0.0065.
Values may be sent and summed in bfloat16 or wider, within the bound.
A program may use at most 64 MiB of HBM per device.

v0:
```python
import jax
import jax.numpy as jnp
from jax import lax
from jax.sharding import PartitionSpec as P

HEADS = 4
KERNEL = 7


def extended(array, sides, width):
    for axis, dim in sides:
        devices, length = (lax.axis_size(axis), array.shape[dim])
        up = [(i, (i + 1) % devices) for i in range(devices - 1)]
        down = [(j, i) for i, j in up]
        last = lax.slice_in_dim(array, length - width, length, axis=dim)
        first = lax.slice_in_dim(array, 0, width, axis=dim)
        before = lax.ppermute(last, axis, up)
        after = lax.ppermute(first, axis, down)
        array = jnp.concatenate([before, array, after], axis=dim)
    return array


def layer_norm(values, gain_vec):
    center = values - jnp.mean(values, axis=-1, keepdims=True)
    spread = jnp.mean(center * center, axis=-1, keepdims=True)
    return center * lax.rsqrt(spread + 1e-06) * gain_vec.astype(jnp.float32)


def mix_members(flat_rows, attn_gain, qkv_weight):
    count, pixels, width = flat_rows.shape
    head_dim = width // HEADS
    normed = layer_norm(flat_rows.astype(jnp.float32), attn_gain).astype(jnp.bfloat16)
    project = jnp.einsum(
        "mpc,jcd->jmpd", normed, qkv_weight, preferred_element_type=jnp.float32
    ).astype(jnp.bfloat16)
    split = project.reshape(3, count, pixels, HEADS, head_dim)
    scores = jnp.einsum(
        "mphd,nphd->hmnp", split[0], split[1], preferred_element_type=jnp.float32
    ) * head_dim ** (-0.5)
    top = jnp.max(scores, axis=2, keepdims=True)
    expo = jnp.exp(scores - top)
    weights = (expo / jnp.sum(expo, axis=2, keepdims=True)).astype(jnp.bfloat16)
    mixed = jnp.einsum(
        "hmnp,nphd->mphd", weights, split[2], preferred_element_type=jnp.float32
    ).astype(jnp.bfloat16)
    return mixed.reshape(count, pixels, width)


def shards(
    fields, conv_weight, conv_gain, mlp_in, mlp_out, layer_scale, attn_gain, qkv_weight, out_weight
):
    members, rows, cols, width = fields.shape
    padded = extended(fields, (("row", 1), ("col", 2)), 3)
    taps = conv_weight.astype(jnp.float32)
    total = jnp.zeros((members, rows, cols, width), jnp.float32)
    for row_tap in range(KERNEL):
        band = padded[:, row_tap : row_tap + rows, :, :]
        partial_row = band[:, :, 0:cols, :].astype(jnp.float32) * taps[row_tap, 0]
        for col_tap in range(1, KERNEL):
            partial_row = (
                partial_row
                + band[:, :, col_tap : col_tap + cols, :].astype(jnp.float32)
                * taps[row_tap, col_tap]
            )
        total = total + partial_row
    normed = layer_norm(total, conv_gain).astype(jnp.bfloat16).reshape(members * rows * cols, width)
    inner = jax.nn.gelu(
        jnp.dot(normed, mlp_in, preferred_element_type=jnp.float32), approximate=True
    ).astype(jnp.bfloat16)
    branch = jnp.dot(inner, mlp_out, preferred_element_type=jnp.float32).reshape(
        members, rows, cols, width
    )
    middle = (fields.astype(jnp.float32) + layer_scale.astype(jnp.float32) * branch).astype(
        jnp.bfloat16
    )
    block = lax.all_to_all(middle, "ens", split_axis=1, concat_axis=0, tiled=True)
    count, block_rows, block_cols, block_width = block.shape
    flat_rows = block.reshape(count, block_rows * block_cols, block_width)
    mixed = mix_members(flat_rows, attn_gain, qkv_weight)
    projected = jnp.einsum("mpc,cd->mpd", mixed, out_weight, preferred_element_type=jnp.float32)
    outcome = (flat_rows.astype(jnp.float32) + projected).astype(jnp.bfloat16)
    outcome = outcome.reshape(count, block_rows, block_cols, block_width)
    gathered = outcome
    gathered = lax.all_to_all(gathered, "ens", split_axis=0, concat_axis=1, tiled=True)
    return gathered


def solution(mesh):
    return jax.shard_map(
        shards,
        mesh=mesh,
        in_specs=(P("ens", ("group", "row"), "col", None), P(), P(), P(), P(), P(), P(), P(), P()),
        out_specs=P("ens", ("group", "row"), "col", None),
        check_vma=False,
    )
```

profile of v0, /device:TPU:0, one launch (start us, length us, event | category | flops | bytes accessed | tf_op | source)
XLA Modules:
  0.0 169.5 jit_solution(12458972681998692937)
XLA Ops:
  1.1 4.8 %collective-permute-start = (bf16[1,3,128,128]{3,2,0,1:T(8,128)(2,1)S(1)}, bf16[1,3,128,128]{3,2,0,1:T(8,128)(2,1)S(1)}, u32[]{:S(2)}, u32[]{:S(2)}) collective-permute-start(bf16[1,3,128,128]{3,2,0,1:T(8,128)(2,1)S(1)} %get-tuple-element.14), channel_id=1, source_target_pairs={{0,2},{1,3},{4,6},{5,7},{8,10},{9,11},{12,14},{13,15},{16,18},{17,... | collective-permute-start | bytes 294920 | tf_op jit(solution)/shard_map/ppermute | solution.py:17
  5.9 1.3 collective-permute-start.1
  8.1 4.3 %collective-permute-done.1 = bf16[1,3,128,128]{3,2,0,1:T(8,128)(2,1)S(1)} collective-permute-done((bf16[1,3,128,128]{3,2,0,1:T(8,128)(2,1)S(1)}, bf16[1,3,128,128]{3,2,0,1:T(8,128)(2,1)S(1)}, u32[]{:S(2)}, u32[]{:S(2)}) %collective-permute-start.1) | collective-permute-done | bytes 98336 | tf_op jit(solution)/shard_map/ppermute | solution.py:18
  13.3 1.3 collective-permute-start.2
  14.6 1.3 collective-permute-start.3
  17.7 1.8 %maximum_maximum_fusion = (bf16[1,38,131,128]{3,2,0,1:T(8,128)(2,1)S(1)}, bf16[1,38,131,128]{3,2,0,1:T(8,128)(2,1)S(1)}) fusion(bf16[1,3,128,128]{3,2,0,1:T(8,128)(2,1)S(1)} %collective-permute-done.1, bf16[1,32,128,128]{3,2,0,1:T(8,128)(2,1)S(1)} %bitcast.150, bf16[1,3,128,128]{3,2,0,1:T(8,128)(2,1)S(1)} %collective-permute-done, ...), kind=kLoop, calls=%fused_computation.34 | loop fusion | flops 10194944 | bytes 3852288 | tf_op jit(solution)/shard_map/concatenate | solution.py:19
  19.5 18.9 %fusion.41 = (f32[32,128]{1,0:T(8,128)S(1)}, f32[1,32,128,128]{3,2,0,1:T(8,128)S(1)}) fusion(f32[128]{0:T(128)S(1)} %get-tuple-element.17, bf16[1,38,131,128]{3,2,0,1:T(8,128)(2,1)S(1)} %get-tuple-element.11, f32[128]{0:T(128)S(1)} %get-tuple-element.18, f32[128]{0:T(128)S(1)} %get-tuple-element.19, f32[128]{0:T(128)S(1)} %get-tuple-element.20, ...), kind=kLoop, calls=%fused_computation.121 | loop fusion | flops 80211968 | bytes 47424000 | tf_op jit(solution)/shard_map/reduce_sum | solution.py:24
  38.5 1.3 multiply_reduce_fusion.1
  41.1 4.4 %fusion.19 = f32[4096,128]{1,0:T(8,128)} fusion(bf16[512,128]{1,0:T(8,128)(2,1)S(1)} %copy-done, bf16[4096,128]{1,0:T(8,128)(2,1)S(1)} %bitcast.159, bf16[128,512]{1,0:T(8,128)(2,1)S(1)} %copy-done.5), kind=kOutput, calls=%fused_computation.29 | convolution fusion | flops 1092616192 | bytes 3407872 | tf_op jit(solution)/shard_map/dot_general | solution.py:70
  45.5 2.9 %fusion.18 = bf16[1,32,128,128]{3,2,0,1:T(8,128)(2,1)} fusion(f32[1,32,128,128]{3,2,0,1:T(8,128)} %bitcast.158, f32[128]{0:T(128)S(1)} %convert_element_type.207, bf16[1,32,128,128]{3,2,1,0:T(8,128)(2,1)S(1)} %copy-done.2), kind=kLoop, calls=%fused_computation.23 | loop fusion | flops 2097152 | bytes 4194816 | tf_op jit(solution)/shard_map/convert_element_type | solution.py:73
  48.4 5.0 %all-to-all-start = ((bf16[1,32,128,128]{3,2,0,1:T(8,128)(2,1)}), bf16[1,32,128,128]{3,2,0,1:T(8,128)(2,1)S(1)}, u32[]{:S(2)}, u32[]{:S(2)}) async-start(bf16[1,32,128,128]{3,2,0,1:T(8,128)(2,1)} %fusion.18), calls=%async_computation | async-start | bytes 2097152 | tf_op jit(solution)/shard_map/all_to_all | solution.py:76
  53.4 26.6 %all-to-all-done = bf16[1,32,128,128]{3,2,0,1:T(8,128)(2,1)S(1)} async-done(((bf16[1,32,128,128]{3,2,0,1:T(8,128)(2,1)}), bf16[1,32,128,128]{3,2,0,1:T(8,128)(2,1)S(1)}, u32[]{:S(2)}, u32[]{:S(2)}) %all-to-all-start) | async-done | bytes 1048608 | tf_op jit(solution)/shard_map/all_to_all | solution.py:76
  80.4 1.3 multiply_reduce_fusion
  81.8 2.1 %convert_bitcast_fusion = bf16[3,4,1024,128]{2,3,0,1:T(8,128)(2,1)S(1)} fusion(f32[128]{0:T(128)S(1)} %convert_element_type.264, f32[4,1024]{1,0:T(4,128)S(1)} %rsqrt.21, f32[4,1024]{1,0:T(4,128)S(1)} %div.25, bf16[3,128,128]{2,1,0:T(8,128)(2,1)S(1)} %copy-done.3, bf16[4,1024,128]{2,1,0:T(8,128)(2,1)S(1)} %bitcast.146), kind=kOutput, calls=%fused_computation.12 | convolution fusion | flops 406847488 | bytes 4325888 | tf_op jit(solution)/shard_map/mpc,jcd->jmpd/dot_general | solution.py:33
  83.8 1.7 fusion.43
  85.5 6.8 %copy.44 = bf16[4,1024,4,32]{3,0,1,2:T(4,128)(2,1)} copy(bf16[4,1024,4,32]{1,3,2,0:T(8,128)(2,1)} %bitcast.156) | data formatting | bytes 2097152 | tf_op jit(solution)/shard_map/squeeze | solution.py:38
  92.3 6.8 %copy.45 = bf16[4,1024,4,32]{3,0,1,2:T(4,128)(2,1)} copy(bf16[4,1024,4,32]{1,3,2,0:T(8,128)(2,1)} %bitcast.155) | data formatting | bytes 2097152 | tf_op jit(solution)/shard_map/squeeze | solution.py:38
  99.1 8.8 %fusion.47 = f32[4,1024,4,4]{3,2,1,0:T(4,128)} fusion(bf16[4,1024,4,32]{3,0,1,2:T(4,128)(2,1)} %copy.44, bf16[4,1024,4,32]{3,0,1,2:T(4,128)(2,1)} %copy.45), kind=kOutput, calls=%fused_computation.126 | convolution fusion | flops 4194304 | bytes 2359296 | tf_op jit(solution)/shard_map/mphd,nphd->hmnp/dot_general | solution.py:37
  107.9 6.8 %copy.46 = f32[4,1024,4,4]{1,2,3,0:T(4,128)S(1)} copy(f32[4,1024,4,4]{3,2,1,0:T(4,128)} %fusion.47) | data formatting | bytes 524288 | tf_op jit(solution)/shard_map/mphd,nphd->hmnp/dot_general | solution.py:37
  115.2 5.5 %copy.48 = bf16[4,4,4,1024]{2,1,0,3:T(4,128)(2,1)} copy(bf16[4,4,4,1024]{3,2,1,0:T(4,128)(2,1)S(1)} %divide_convert_fusion) | data formatting | bytes 262144 | tf_op jit(solution)/shard_map/convert_element_type | solution.py:42
  120.6 5.3 %copy.47 = bf16[4,1024,4,32]{3,0,2,1:T(4,128)(2,1)} copy(bf16[4,1024,4,32]{1,3,2,0:T(8,128)(2,1)S(1)} %bitcast.154) | data formatting | bytes 2097152 | tf_op jit(solution)/shard_map/squeeze | solution.py:44
  126.0 8.3 %fusion.9 = bf16[4,1024,4,32]{3,0,2,1:T(4,128)(2,1)} fusion(bf16[4,1024,4,32]{3,0,2,1:T(4,128)(2,1)} %copy.47, bf16[4,4,4,1024]{2,1,0,3:T(4,128)(2,1)} %copy.48), kind=kOutput, calls=%fused_computation.11 | convolution fusion | flops 4718592 | bytes 2228224 | tf_op jit(solution)/shard_map/hmnp,nphd->mphd/dot_general | solution.py:43
  134.3 5.5 %copy.49 = bf16[4,1024,4,32]{1,3,2,0:T(8,128)(2,1)S(1)} copy(bf16[4,1024,4,32]{3,0,2,1:T(4,128)(2,1)} %fusion.9) | data formatting | bytes 2097152 | tf_op jit(solution)/shard_map/convert_element_type | solution.py:45
  140.3 28.2 %all_to_all.21 = bf16[4,8,128,128]{3,2,1,0:T(8,128)(2,1)S(1)} all-to-all(bf16[4,8,128,128]{3,2,1,0:T(8,128)(2,1)S(1)} %bitcast.153), channel_id=1, replica_groups=mesh['group'=2,'ens'=4,'row'=2,'col'=2] {'ens'}, dimensions={0} | all-to-all | bytes 2097152 | tf_op jit(solution)/shard_map/all_to_all | solution.py:84
  (38 shorter events, 8.2 us)
Async XLA Ops:
  0.0 41.1 %copy-start = (bf16[512,128]{1,0:T(8,128)(2,1)S(1)}, bf16[512,128]{1,0:T(8,128)(2,1)}, u32[]{:S(2)}) copy-start(bf16[512,128]{1,0:T(8,128)(2,1)} %param.13) | copy-start | bytes 393220
  0.0 17.7 %copy-start.1 = (bf16[1,32,128,128]{3,2,1,0:T(8,128)(2,1)S(1)}, bf16[1,32,128,128]{3,2,1,0:T(8,128)(2,1)}, u32[]{:S(2)}) copy-start(bf16[1,32,128,128]{3,2,1,0:T(8,128)(2,1)} %param.9) | copy-start | bytes 3145732
  1.1 7.0 %collective-permute-start = (bf16[1,3,128,128]{3,2,0,1:T(8,128)(2,1)S(1)}, bf16[1,3,128,128]{3,2,0,1:T(8,128)(2,1)S(1)}, u32[]{:S(2)}, u32[]{:S(2)}) collective-permute-start(bf16[1,3,128,128]{3,2,0,1:T(8,128)(2,1)S(1)} %get-tuple-element.14), channel_id=1, source_target_pairs={{0,2},{1,3},{4,6},{5,7},{8,10},{9,11},{12,14},{13,15},{16,18},{17,... | collective-permute-start | bytes 294920 | tf_op jit(solution)/shard_map/ppermute | solution.py:17
  5.9 6.5 %collective-permute-start.1 = (bf16[1,3,128,128]{3,2,0,1:T(8,128)(2,1)S(1)}, bf16[1,3,128,128]{3,2,0,1:T(8,128)(2,1)S(1)}, u32[]{:S(2)}, u32[]{:S(2)}) collective-permute-start(bf16[1,3,128,128]{3,2,0,1:T(8,128)(2,1)S(1)} %get-tuple-element.15), channel_id=1, source_target_pairs={{2,0},{3,1},{6,4},{7,5},{10,8},{11,9},{14,12},{15,13},{18,16},{19,... | collective-permute-start | bytes 294920 | tf_op jit(solution)/shard_map/ppermute | solution.py:18
  13.3 3.9 %collective-permute-start.2 = (bf16[1,38,3,128]{3,2,0,1:T(4,128)(2,1)S(1)}, bf16[1,38,3,128]{3,2,0,1:T(4,128)(2,1)S(1)}, u32[]{:S(2)}, u32[]{:S(2)}) collective-permute-start(bf16[1,38,3,128]{3,2,0,1:T(4,128)(2,1)S(1)} %get-tuple-element.12), channel_id=1, source_target_pairs={{0,1},{2,3},{4,5},{6,7},{8,9},{10,11},{12,13},{14,15},{16,17},{18,... | collective-permute-start | bytes 87560 | tf_op jit(solution)/shard_map/ppermute | solution.py:17
  14.6 3.1 %collective-permute-start.3 = (bf16[1,38,3,128]{3,2,0,1:T(4,128)(2,1)S(1)}, bf16[1,38,3,128]{3,2,0,1:T(4,128)(2,1)S(1)}, u32[]{:S(2)}, u32[]{:S(2)}) collective-permute-start(bf16[1,38,3,128]{3,2,0,1:T(4,128)(2,1)S(1)} %get-tuple-element.13), channel_id=1, source_target_pairs={{1,0},{3,2},{5,4},{7,6},{9,8},{11,10},{13,12},{15,14},{17,16},{19,... | collective-permute-start | bytes 87560 | tf_op jit(solution)/shard_map/ppermute | solution.py:18
  39.8 1.3 copy-start.5
  41.1 4.5 %copy-start.2 = (bf16[1,32,128,128]{3,2,1,0:T(8,128)(2,1)S(1)}, bf16[1,32,128,128]{3,2,1,0:T(8,128)(2,1)}, u32[]{:S(2)}) copy-start(bf16[1,32,128,128]{3,2,1,0:T(8,128)(2,1)} %param.9) | copy-start | bytes 3145732
  48.4 5.0 %copy-start.6 = (bf16[128]{0:T(256)(128)(2,1)S(1)}, bf16[128]{0:T(256)(128)(2,1)}, u32[]{:S(2)}) copy-start(bf16[128]{0:T(256)(128)(2,1)} %param.15) | copy-start | bytes 772
  48.4 33.3 %copy-start.3 = (bf16[3,128,128]{2,1,0:T(8,128)(2,1)S(1)}, bf16[3,128,128]{2,1,0:T(8,128)(2,1)}, u32[]{:S(2)}) copy-start(bf16[3,128,128]{2,1,0:T(8,128)(2,1)} %param.16) | copy-start | bytes 294916
  48.4 31.6 %all-to-all-start = ((bf16[1,32,128,128]{3,2,0,1:T(8,128)(2,1)}), bf16[1,32,128,128]{3,2,0,1:T(8,128)(2,1)S(1)}, u32[]{:S(2)}, u32[]{:S(2)}) async-start(bf16[1,32,128,128]{3,2,0,1:T(8,128)(2,1)} %fusion.18), calls=%async_computation | async-start | bytes 2097152 | tf_op jit(solution)/shard_map/all_to_all | solution.py:76
  134.3 5.5 %copy-start.4 = (bf16[128,128]{1,0:T(8,128)(2,1)S(1)}, bf16[128,128]{1,0:T(8,128)(2,1)}, u32[]{:S(2)}) copy-start(bf16[128,128]{1,0:T(8,128)(2,1)} %param.17) | copy-start | bytes 98308
where the time goes:
time: 171 us; the launch traced here: 170 us
  local copies, waits for them, and re-layouts  40.5 us (24%)
  waiting for transfers between devices  31.5 us (18%)
  other arithmetic  31.2 us (18%)
  blocking collectives  28.2 us (16%)
  matrix products  24.2 us (14%)
  starting transfers between devices  13.7 us (8%)
    all_to_all x1, blocking collectives, shards(): lax.all_to_all(gathered, 'ens', split_axis=0, concat_axis=1, tiled=True)  28.2 us
    all_to_all x1, waiting for transfers between devices, shards(): lax.all_to_all(middle, 'ens', split_axis=1, concat_axis=0, tiled=True)  26.6 us
    reduce_sum x2, other arithmetic, layer_norm(): center = values - jnp.mean(values, axis=-1, keepdims=True)  19.3 us
    dot_general x1, matrix products, mix_members(): jnp.einsum('mphd,nphd->hmnp', split[0], split[1], preferred_element_type=...  8.83 us
    dot_general x1, matrix products, mix_members(): jnp.einsum('hmnp,nphd->mphd', weights, split[2], preferred_element_type=j...  8.34 us
    dot_general x1, local copies, waits for them, and re-layouts, mix_members(): jnp.einsum('mphd,nphd->hmnp', split[0], split[1], preferred_element_type=...  6.82 us
    squeeze x1, local copies, waits for them, and re-layouts, mix_members(): split[1]  6.79 us
    squeeze x1, local copies, waits for them, and re-layouts, mix_members(): split[0]  6.77 us
  transfers between devices with their start and end apart: 5, of which 4 were waited for; matrix products, arithmetic and copies ran while one was open for 1% of the time, Pallas kernels for 0%

commit v1 on v0

v1 whole, which is shorter than its diff:
```python
import functools
import math

import jax
import jax.numpy as jnp
from jax import lax
from jax.experimental import pallas as pl
from jax.experimental.pallas import tpu as pltpu
from jax.sharding import PartitionSpec as P

HEADS = 4
KERNEL = 7
HALO = KERNEL // 2
PAD = 16
MESH = pl.DeviceIdType.MESH
F32 = jnp.float32
BF16 = jnp.bfloat16
SIDES = [(a, b) for a in (-1, 0, 1) for b in (-1, 0, 1) if (a, b) != (0, 0)]


def norm(values, gain):
    center = values - jnp.mean(values, axis=-1, keepdims=True)
    spread = jnp.mean(center * center, axis=-1, keepdims=True)
    return (center * lax.rsqrt(spread + 1e-06) * gain).astype(BF16)


def gelu(h):
    inner = h * (0.7978845608028654 + 0.035677408136300125 * (h * h))
    return (0.5 * h) * (1.0 + jnp.tanh(inner))


def kernel(
    n, row_n, col_n, sub,
    fields, conv_weight, conv_gain, mlp_in, mlp_out, layer_scale, attn_gain, qkv, out_weight,
    out,
    pad, taps, conv, mid, recv, back, q_s, k_s, v_s, halo_rows, halo_cols, halo_corner,
    halo_send, halo_recv, send1, recv1, send2, recv2,
):
    _, rows, cols, width = fields.shape
    share = rows // n
    steps = share // sub
    me = lax.axis_index("ens")
    row_i = lax.axis_index("row")
    col_i = lax.axis_index("col")
    barrier = pltpu.get_barrier_semaphore()

    def exists(a, b):
        ok = None
        for d, i, size in ((a, row_i, row_n), (b, col_i, col_n)):
            if d == 0:
                continue
            one = i > 0 if d < 0 else i < size - 1
            ok = one if ok is None else jnp.logical_and(ok, one)
        return ok

    def other(k):
        return lax.rem(me + 1 + k, n)

    for a, b in SIDES:
        @pl.when(exists(a, b))
        def _(a=a, b=b):
            pl.semaphore_signal(
                barrier, inc=1, device_id={"row": row_i + a, "col": col_i + b}, device_id_type=MESH
            )

    @pl.loop(0, n - 1)
    def _(k):
        pl.semaphore_signal(barrier, inc=1, device_id={"ens": other(k)}, device_id_type=MESH)

    def around(i, size):
        return jnp.where(i > 0, 1, 0) + jnp.where(i < size - 1, 1, 0) + 1

    pl.semaphore_wait(barrier, around(row_i, row_n) * around(col_i, col_n) + (n - 2))

    def halo_ref(a, b):
        if b == 0:
            return halo_rows.at[0 if a < 0 else 1]
        if a == 0:
            return halo_cols.at[0 if b < 0 else 1]
        return halo_corner.at[(0 if a < 0 else 2) + (0 if b < 0 else 1)]

    def halo_copy(a, b):
        r = slice(0, rows) if a == 0 else (slice(0, HALO) if a < 0 else slice(rows - HALO, rows))
        c = slice(0, cols) if b == 0 else (slice(0, PAD) if b < 0 else slice(cols - PAD, cols))
        return pltpu.make_async_remote_copy(
            src_ref=fields.at[0, r, c, :],
            dst_ref=halo_ref(-a, -b),
            send_sem=halo_send.at[SIDES.index((a, b))],
            recv_sem=halo_recv.at[SIDES.index((-a, -b))],
            device_id={"row": row_i + a, "col": col_i + b},
            device_id_type=MESH,
        )

    for a, b in SIDES:
        @pl.when(exists(a, b))
        def _(a=a, b=b):
            halo_copy(a, b).start()

    for a in range(KERNEL):
        taps[a, 0:KERNEL, :] = conv_weight[a].astype(F32)

    @pl.loop(0, rows)
    def _(r):
        pad[HALO + r, PAD : PAD + cols, :] = fields[0, r].astype(F32)

    def spot(a, b):
        r = slice(HALO, HALO + rows) if a == 0 else (
            slice(0, HALO) if a < 0 else slice(HALO + rows, 2 * HALO + rows))
        c = slice(PAD, PAD + cols) if b == 0 else (
            slice(0, PAD) if b < 0 else slice(PAD + cols, 2 * PAD + cols))
        return r, c

    for a, b in SIDES:
        here = exists(a, b)
        r, c = spot(a, b)

        @pl.when(here)
        def _(a=a, b=b, r=r, c=c):
            pltpu.make_async_remote_copy(
                src_ref=halo_ref(a, b),
                dst_ref=halo_ref(a, b),
                send_sem=halo_send.at[SIDES.index((a, b))],
                recv_sem=halo_recv.at[SIDES.index((a, b))],
                device_id={"row": row_i + a, "col": col_i + b},
                device_id_type=MESH,
            ).wait_recv()
            pad[r, c, :] = halo_ref(a, b)[...].astype(F32)

        @pl.when(jnp.logical_not(here))
        def _(r=r, c=c):
            pad[r, c, :] = jnp.zeros((r.stop - r.start, c.stop - c.start, width), F32)

    gain1 = conv_gain[...].astype(F32).reshape(1, width)
    gain2 = attn_gain[...].astype(F32).reshape(1, width)
    scale = layer_scale[...].astype(F32).reshape(1, width)
    head = width // HEADS
    ones = (
        lax.broadcasted_iota(jnp.int32, (width, width), 0) // head
        == lax.broadcasted_iota(jnp.int32, (width, width), 1) // head
    ).astype(F32).astype(BF16)
    factor = head**-0.5 * math.log2(math.e)

    def to_mixer(s, d):
        return pltpu.make_async_remote_copy(
            src_ref=mid.at[s, d],
            dst_ref=recv.at[s, me],
            send_sem=send1.at[s, d],
            recv_sem=recv1.at[s, me],
            device_id={"ens": d},
            device_id_type=MESH,
        )

    def from_member(s, d):
        return pltpu.make_async_remote_copy(
            src_ref=mid.at[s, d],
            dst_ref=recv.at[s, d],
            send_sem=send1.at[s, d],
            recv_sem=recv1.at[s, d],
            device_id={"ens": d},
            device_id_type=MESH,
        )

    def to_member(s, d):
        return pltpu.make_async_remote_copy(
            src_ref=back.at[s, d],
            dst_ref=out.at[0, pl.ds(me * share + s * sub, sub)],
            send_sem=send2.at[s, d],
            recv_sem=recv2.at[s, me],
            device_id={"ens": d},
            device_id_type=MESH,
        )

    def from_mixer(s, d):
        return pltpu.make_async_remote_copy(
            src_ref=back.at[s, d],
            dst_ref=out.at[0, pl.ds(d * share + s * sub, sub)],
            send_sem=send2.at[s, d],
            recv_sem=recv2.at[s, d],
            device_id={"ens": d},
            device_id_type=MESH,
        )

    def block(s, k):
        d = other(k)
        first = d * share + s * sub

        @pl.loop(0, cols // 16)
        def _(j):
            c0 = j * 16
            acc = [jnp.zeros((16, width), F32) for _ in range(sub)]
            for b in range(KERNEL):
                lines = [
                    pad[first + r, pl.ds(c0 + (PAD - HALO + b), 16), :]
                    for r in range(sub + KERNEL - 1)
                ]
                for a in range(KERNEL):
                    w = taps[a, b : b + 1, :]
                    acc = [acc[r] + lines[r + a] * w for r in range(sub)]
            for r in range(sub):
                conv[r, pl.ds(pl.multiple_of(c0, 16), 16), :] = acc[r]

        for r in range(sub):
            normed = norm(conv[r], gain1)
            h = jnp.dot(normed, mlp_in[...], preferred_element_type=F32)
            inner = gelu(h).astype(BF16)
            branch = jnp.dot(inner, mlp_out[...], preferred_element_type=F32)
            mid[s, d, r] = (fields[0, first + r].astype(F32) + scale * branch).astype(BF16)

        @pl.when(k < n - 1)
        def _():
            to_mixer(s, d).start()

        @pl.when(k == n - 1)
        def _():
            recv[s, me] = mid[s, me]

    few = n <= 8

    def each_member(body):
        if few:
            for m in range(n):
                body(m)
        else:
            pl.loop(0, n)(body)

    def mix(s):
        @pl.loop(0, n - 1)
        def _(k):
            from_member(s, other(k)).wait_recv()

        @pl.loop(0, sub)
        def _(r):
            def project(m):
                normed = norm(recv[s, m, r].astype(F32), gain2)
                q_s[m] = jnp.dot(normed, qkv[0], preferred_element_type=F32).astype(BF16)
                k_s[m] = jnp.dot(normed, qkv[1], preferred_element_type=F32).astype(BF16)
                v_s[m] = jnp.dot(normed, qkv[2], preferred_element_type=F32).astype(BF16)

            def attend(m):
                def score(j):
                    prod = q_s[m].astype(F32) * k_s[j].astype(F32)
                    return jnp.dot(prod.astype(BF16), ones, preferred_element_type=F32)

                if few:
                    scores = [score(j) for j in range(n)]
                    top = functools.reduce(jnp.maximum, scores)
                    den, acc = None, None
                    for j in range(n):
                        e = jnp.exp2((scores[j] - top) * factor)
                        term = e * v_s[j].astype(F32)
                        den = e if den is None else den + e
                        acc = term if acc is None else acc + term
                else:
                    def more(j, carry):
                        top, den, acc = carry
                        sc = score(j)
                        now = jnp.maximum(top, sc)
                        keep = jnp.exp2((top - now) * factor)
                        e = jnp.exp2((sc - now) * factor)
                        return now, den * keep + e, acc * keep + e * v_s[j].astype(F32)

                    _, den, acc = lax.fori_loop(
                        1, n, more,
                        (score(0), jnp.ones((cols, width), F32), v_s[0].astype(F32)),
                    )
                mixed = (acc / den).astype(BF16)
                proj = jnp.dot(mixed, out_weight[...], preferred_element_type=F32)
                back[s, m, r] = (recv[s, m, r].astype(F32) + proj).astype(BF16)

            each_member(project)
            each_member(attend)

        @pl.loop(0, n - 1)
        def _(k):
            to_member(s, other(k)).start()

        out[0, pl.ds(me * share + s * sub, sub)] = back[s, me]

    @pl.loop(0, steps + 1)
    def _(s):
        @pl.when(s < steps)
        def _():
            pl.loop(0, n)(lambda k: block(s, k))

        @pl.when(s >= 1)
        def _():
            mix(s - 1)

    for a, b in SIDES:
        @pl.when(exists(a, b))
        def _(a=a, b=b):
            halo_copy(a, b).wait_send()

    @pl.loop(0, steps)
    def _(s):
        @pl.loop(0, n - 1)
        def _(k):
            d = other(k)
            to_mixer(s, d).wait_send()
            to_member(s, d).wait_send()
            from_mixer(s, d).wait_recv()


SUB = 4


def shards(n, row_n, col_n, *args):
    fields = args[0]
    _, rows, cols, width = fields.shape
    share = rows // n
    sub = math.gcd(share, SUB)
    steps = share // sub
    vmem = pl.BlockSpec(memory_space=pltpu.VMEM)
    dma = pltpu.SemaphoreType.DMA
    blocks = (steps, n, sub, cols, width)
    return pl.pallas_call(
        functools.partial(kernel, n, row_n, col_n, sub),
        out_shape=jax.ShapeDtypeStruct(fields.shape, fields.dtype),
        in_specs=[vmem] * len(args),
        out_specs=vmem,
        scratch_shapes=[
            pltpu.VMEM((rows + 2 * HALO, cols + 2 * PAD, width), F32),
            pltpu.VMEM((KERNEL, 8, width), F32),
            pltpu.VMEM((sub, cols, width), F32),
            pltpu.VMEM(blocks, BF16),
            pltpu.VMEM(blocks, BF16),
            pltpu.VMEM(blocks, BF16),
            pltpu.VMEM((n, cols, width), BF16),
            pltpu.VMEM((n, cols, width), BF16),
            pltpu.VMEM((n, cols, width), BF16),
            pltpu.VMEM((2, HALO, cols, width), BF16),
            pltpu.VMEM((2, rows, PAD, width), BF16),
            pltpu.VMEM((4, HALO, PAD, width), BF16),
            dma((8,)),
            dma((8,)),
            dma((steps, n)),
            dma((steps, n)),
            dma((steps, n)),
            dma((steps, n)),
        ],
        compiler_params=pltpu.CompilerParams(
            collective_id=0, has_side_effects=True, vmem_limit_bytes=48 * 1024 * 1024
        ),
    )(*args)


def solution(mesh):
    size = mesh.shape
    return jax.shard_map(
        functools.partial(shards, size["ens"], size["row"], size["col"]),
        mesh=mesh,
        in_specs=(P("ens", ("group", "row"), "col", None), P(), P(), P(), P(), P(), P(), P(), P()),
        out_specs=P("ens", ("group", "row"), "col", None),
        check_vma=False,
    )
```

time: 171 us -> 66.4 us (0.39)
  Pallas kernels: 0 us -> 57 us
  local copies, waits for them, and re-layouts: 40.5 us -> 8.33 us
  waiting for transfers between devices: 31.5 us -> 0 us
  other arithmetic: 31.2 us -> 0 us
  blocking collectives: 28.2 us -> 0 us
  matrix products: 24.2 us -> 0 us
  starting transfers between devices: 13.7 us -> 0 us
    pallas_call x0 -> x1, Pallas kernels: none -> 57 us  [shards(): pl.pallas_call(functools.partial(kernel, n, row_n, col_n, sub), out_shape...]
    all_to_all x1 -> x0, blocking collectives: 28.2 us -> none  [shards(): lax.all_to_all(gathered, 'ens', split_axis=0, concat_axis=1, tiled=True)]
    all_to_all x1 -> x0, waiting for transfers between devices: 26.6 us -> none  [shards(): lax.all_to_all(middle, 'ens', split_axis=1, concat_axis=0, tiled=True)]
    dot_general x5 -> x0, matrix products: 24.2 us -> none  [the longest x1 8.83 us: mix_members(): jnp.einsum('mphd,nphd->hmnp', split[0], split[1], preferred_element_type=...]
    reduce_sum x4 -> x0, other arithmetic: 21.9 us -> none  [the longest x2 19.3 us: layer_norm(): center = values - jnp.mean(values, axis=-1, keepdims=True)]
    squeeze x3 -> x0, local copies, waits for them, and re-layouts: 18.9 us -> none  [the longest x1 6.79 us: mix_members(): split[1]]
    convert_element_type x2 -> x0, local copies, waits for them, and re-layouts: 11 us -> none  [the longest x1 5.51 us: mix_members(): mixed = jnp.einsum('hmnp,nphd->mphd', weights, split[2], preferred_elemen...]
    ppermute x4 -> x0, starting transfers between devices: 8.72 us -> none  [the longest x2 6.14 us: extended(): before = lax.ppermute(last, axis, up)]
  transfers between devices with their start and end apart: 5 -> 0, of which waited for: 4 -> 0; matrix products, arithmetic and copies ran while one was open for 1% -> 0% of each run, Pallas kernels for 0% -> 0%
where the time goes in v1:
time: 66.4 us; the launch traced here: 65.4 us
  Pallas kernels  57 us (86%)
  local copies, waits for them, and re-layouts  8.33 us (13%)
    pallas_call x1, Pallas kernels, shards(): pl.pallas_call(functools.partial(kernel, n, row_n, col_n, sub), out_shape...  57 us
    unnamed x19, local copies, waits for them, and re-layouts  8.33 us

profile of v1, /device:TPU:0, one launch (start us, length us, event | category | flops | bytes accessed | tf_op | source)
XLA Modules:
  0.0 65.4 jit_solution(2783957098250857410)
XLA Ops:
  0.0 0.0 copy-start
  0.0 1.2 %copy-done = bf16[1,32,128,128]{3,2,1,0:T(8,128)(2,1)S(1)} copy-done((bf16[1,32,128,128]{3,2,1,0:T(8,128)(2,1)S(1)}, bf16[1,32,128,128]{3,2,1,0:T(8,128)(2,1)}, u32[]{:S(2)}) %copy-start) | copy-done | bytes 1048600
  1.2 0.0 copy-start.1
  1.2 0.9 %copy-done.1 = bf16[128,512]{1,0:T(8,128)(2,1)S(1)} copy-done((bf16[128,512]{1,0:T(8,128)(2,1)S(1)}, bf16[128,512]{1,0:T(8,128)(2,1)}, u32[]{:S(2)}) %copy-start.1) | copy-done | bytes 131096
  2.1 0.0 copy-start.2
  2.1 0.9 %copy-done.2 = bf16[512,128]{1,0:T(8,128)(2,1)S(1)} copy-done((bf16[512,128]{1,0:T(8,128)(2,1)S(1)}, bf16[512,128]{1,0:T(8,128)(2,1)}, u32[]{:S(2)}) %copy-start.2) | copy-done | bytes 131096
  3.0 0.0 copy-start.3
  3.0 0.9 %copy-done.3 = bf16[3,128,128]{2,1,0:T(8,128)(2,1)S(1)} copy-done((bf16[3,128,128]{2,1,0:T(8,128)(2,1)S(1)}, bf16[3,128,128]{2,1,0:T(8,128)(2,1)}, u32[]{:S(2)}) %copy-start.3) | copy-done | bytes 98328
  3.9 0.0 copy-start.4
  3.9 0.8 %copy-done.4 = bf16[128,128]{1,0:T(8,128)(2,1)S(1)} copy-done((bf16[128,128]{1,0:T(8,128)(2,1)S(1)}, bf16[128,128]{1,0:T(8,128)(2,1)}, u32[]{:S(2)}) %copy-start.4) | copy-done | bytes 32792
  4.7 0.0 copy-start.5
  4.7 0.7 %copy-done.5 = bf16[7,7,128]{2,1,0:T(8,128)(2,1)S(1)} copy-done((bf16[7,7,128]{2,1,0:T(8,128)(2,1)S(1)}, bf16[7,7,128]{2,1,0:T(8,128)(2,1)}, u32[]{:S(2)}) %copy-start.5) | copy-done | bytes 12568
  5.4 0.0 copy-start.6
  5.4 0.7 copy-done.6
  6.1 0.0 copy-start.7
  6.1 0.7 copy-done.7
  6.7 0.0 copy-start.8
  6.7 0.7 copy-done.8
  7.4 57.0 %shard_map.91 = bf16[1,32,128,128]{3,2,1,0:T(8,128)(2,1)S(1)} custom-call(bf16[1,32,128,128]{3,2,1,0:T(8,128)(2,1)S(1)} %copy-done, bf16[7,7,128]{2,1,0:T(8,128)(2,1)S(1)} %copy-done.5, bf16[128]{0:T(256)(128)(2,1)S(1)} %copy-done.6, bf16[128,512]{1,0:T(8,128)(2,1)S(1)} %copy-done.1, bf16[512,128]{1,0:T(8,128)(2,1)S(1)} %copy-done.2, ...), custom_call_target="tpu_custom_call" | custom-call | tf_op jit(solution)/shard_map/pallas_call | solution.py:316
  64.4 1.0 %copy.11 = bf16[1,32,128,128]{3,2,1,0:T(8,128)(2,1)} copy(bf16[1,32,128,128]{3,2,1,0:T(8,128)(2,1)S(1)} %shard_map.91) | data formatting | bytes 2097152
Async XLA Ops:
  0.0 1.2 %copy-start = (bf16[1,32,128,128]{3,2,1,0:T(8,128)(2,1)S(1)}, bf16[1,32,128,128]{3,2,1,0:T(8,128)(2,1)}, u32[]{:S(2)}) copy-start(bf16[1,32,128,128]{3,2,1,0:T(8,128)(2,1)} %fields.1) | copy-start | bytes 3145732
  1.2 0.9 %copy-start.1 = (bf16[128,512]{1,0:T(8,128)(2,1)S(1)}, bf16[128,512]{1,0:T(8,128)(2,1)}, u32[]{:S(2)}) copy-start(bf16[128,512]{1,0:T(8,128)(2,1)} %mlp_in.1) | copy-start | bytes 393220
  2.1 0.9 %copy-start.2 = (bf16[512,128]{1,0:T(8,128)(2,1)S(1)}, bf16[512,128]{1,0:T(8,128)(2,1)}, u32[]{:S(2)}) copy-start(bf16[512,128]{1,0:T(8,128)(2,1)} %mlp_out.1) | copy-start | bytes 393220
  3.0 0.9 %copy-start.3 = (bf16[3,128,128]{2,1,0:T(8,128)(2,1)S(1)}, bf16[3,128,128]{2,1,0:T(8,128)(2,1)}, u32[]{:S(2)}) copy-start(bf16[3,128,128]{2,1,0:T(8,128)(2,1)} %qkv.1) | copy-start | bytes 294916
  3.9 0.8 %copy-start.4 = (bf16[128,128]{1,0:T(8,128)(2,1)S(1)}, bf16[128,128]{1,0:T(8,128)(2,1)}, u32[]{:S(2)}) copy-start(bf16[128,128]{1,0:T(8,128)(2,1)} %out_weight.1) | copy-start | bytes 98308
  4.7 0.7 %copy-start.5 = (bf16[7,7,128]{2,1,0:T(8,128)(2,1)S(1)}, bf16[7,7,128]{2,1,0:T(8,128)(2,1)}, u32[]{:S(2)}) copy-start(bf16[7,7,128]{2,1,0:T(8,128)(2,1)} %conv_weight.1) | copy-start | bytes 37636
  5.4 0.7 %copy-start.6 = (bf16[128]{0:T(256)(128)(2,1)S(1)}, bf16[128]{0:T(256)(128)(2,1)}, u32[]{:S(2)}) copy-start(bf16[128]{0:T(256)(128)(2,1)} %conv_gain.1) | copy-start | bytes 772
  6.1 0.7 %copy-start.7 = (bf16[128]{0:T(256)(128)(2,1)S(1)}, bf16[128]{0:T(256)(128)(2,1)}, u32[]{:S(2)}) copy-start(bf16[128]{0:T(256)(128)(2,1)} %layer_scale.1) | copy-start | bytes 772
  6.7 0.7 %copy-start.8 = (bf16[128]{0:T(256)(128)(2,1)S(1)}, bf16[128]{0:T(256)(128)(2,1)}, u32[]{:S(2)}) copy-start(bf16[128]{0:T(256)(128)(2,1)} %attn_gain.1) | copy-start | bytes 772

commit v2 on v1

--- a/solution.py
+++ b/solution.py
@@ -31,17 +31,28 @@
 
 def kernel(
     n, row_n, col_n, sub,
-    fields, conv_weight, conv_gain, mlp_in, mlp_out, layer_scale, attn_gain, qkv, out_weight,
-    out,
-    pad, taps, conv, mid, recv, back, q_s, k_s, v_s, halo_rows, halo_cols, halo_corner,
+    fields_hbm, *refs,
+):
+    count = 8
+    weights_hbm, out, weights = refs[:count], refs[count], refs[count + 1 : 2 * count + 1]
+    fields, load = refs[2 * count + 1 : 2 * count + 3]
+    conv_weight, conv_gain, mlp_in, mlp_out, layer_scale, attn_gain, qkv, out_weight = weights
+    (
+    pad, taps, conv, mid, recv, back, q_s, k_s, v_s, qkv_s, halo_rows, halo_cols, halo_corner,
     halo_send, halo_recv, send1, recv1, send2, recv2,
-):
+    ) = refs[2 * count + 3 :]
     _, rows, cols, width = fields.shape
     share = rows // n
     steps = share // sub
     me = lax.axis_index("ens")
     row_i = lax.axis_index("row")
     col_i = lax.axis_index("col")
+    loads = [
+        pltpu.make_async_copy(src, dst, load.at[i])
+        for i, (src, dst) in enumerate(zip((fields_hbm, *weights_hbm), (fields, *weights)))
+    ]
+    for copy in loads:
+        copy.start()
     barrier = pltpu.get_barrier_semaphore()
 
     def exists(a, b):
@@ -53,8 +64,15 @@
             ok = one if ok is None else jnp.logical_and(ok, one)
         return ok
 
+    half = n // 2 if n % 2 == 0 else n
+
     def other(k):
-        return lax.rem(me + 1 + k, n)
+        if n % 2:
+            return lax.rem(me + 1 + k, n)
+        side = me // half
+        far = (1 - side) * half + lax.rem(me + k, half)
+        near = side * half + lax.rem(me + 1 + k, half)
+        return jnp.where(k < half, far, near)
 
     for a, b in SIDES:
         @pl.when(exists(a, b))
@@ -83,7 +101,7 @@
         r = slice(0, rows) if a == 0 else (slice(0, HALO) if a < 0 else slice(rows - HALO, rows))
         c = slice(0, cols) if b == 0 else (slice(0, PAD) if b < 0 else slice(cols - PAD, cols))
         return pltpu.make_async_remote_copy(
-            src_ref=fields.at[0, r, c, :],
+            src_ref=fields_hbm.at[0, r, c, :],
             dst_ref=halo_ref(-a, -b),
             send_sem=halo_send.at[SIDES.index((a, b))],
             recv_sem=halo_recv.at[SIDES.index((-a, -b))],
@@ -96,6 +114,10 @@
         def _(a=a, b=b):
             halo_copy(a, b).start()
 
+    for copy in loads:
+        copy.wait()
+    for j in range(3):
+        qkv_s[:, j * width : (j + 1) * width] = qkv[j]
     for a in range(KERNEL):
         taps[a, 0:KERNEL, :] = conv_weight[a].astype(F32)
 
@@ -135,47 +157,47 @@
     scale = layer_scale[...].astype(F32).reshape(1, width)
     head = width // HEADS
     ones = (
-        lax.broadcasted_iota(jnp.int32, (width, width), 0) // head
-        == lax.broadcasted_iota(jnp.int32, (width, width), 1) // head
+        lax.broadcasted_iota(jnp.int32, (2 * width, 2 * width), 0) // head
+        == lax.broadcasted_iota(jnp.int32, (2 * width, 2 * width), 1) // head
     ).astype(F32).astype(BF16)
     factor = head**-0.5 * math.log2(math.e)
 
-    def to_mixer(s, d):
-        return pltpu.make_async_remote_copy(
-            src_ref=mid.at[s, d],
-            dst_ref=recv.at[s, me],
-            send_sem=send1.at[s, d],
-            recv_sem=recv1.at[s, me],
+    def to_mixer(s, d, r):
+        return pltpu.make_async_remote_copy(
+            src_ref=mid.at[s, d, r],
+            dst_ref=recv.at[s, me, r],
+            send_sem=send1.at[s, d, r],
+            recv_sem=recv1.at[s, me, r],
             device_id={"ens": d},
             device_id_type=MESH,
         )
 
-    def from_member(s, d):
-        return pltpu.make_async_remote_copy(
-            src_ref=mid.at[s, d],
-            dst_ref=recv.at[s, d],
-            send_sem=send1.at[s, d],
-            recv_sem=recv1.at[s, d],
+    def from_member(s, d, r):
+        return pltpu.make_async_remote_copy(
+            src_ref=mid.at[s, d, r],
+            dst_ref=recv.at[s, d, r],
+            send_sem=send1.at[s, d, r],
+            recv_sem=recv1.at[s, d, r],
             device_id={"ens": d},
             device_id_type=MESH,
         )
 
-    def to_member(s, d):
-        return pltpu.make_async_remote_copy(
-            src_ref=back.at[s, d],
-            dst_ref=out.at[0, pl.ds(me * share + s * sub, sub)],
-            send_sem=send2.at[s, d],
-            recv_sem=recv2.at[s, me],
+    def to_member(s, d, r):
+        return pltpu.make_async_remote_copy(
+            src_ref=back.at[s, d, r],
+            dst_ref=out.at[0, me * share + s * sub + r],
+            send_sem=send2.at[s, d, r],
+            recv_sem=recv2.at[s, me, r],
             device_id={"ens": d},
             device_id_type=MESH,
         )
 
-    def from_mixer(s, d):
-        return pltpu.make_async_remote_copy(
-            src_ref=back.at[s, d],
-            dst_ref=out.at[0, pl.ds(d * share + s * sub, sub)],
-            send_sem=send2.at[s, d],
-            recv_sem=recv2.at[s, d],
+    def from_mixer(s, d, r):
+        return pltpu.make_async_remote_copy(
+            src_ref=back.at[s, d, r],
+            dst_ref=out.at[0, d * share + s * sub + r],
+            send_sem=send2.at[s, d, r],
+            recv_sem=recv2.at[s, d, r],
             device_id={"ens": d},
             device_id_type=MESH,
         )
@@ -199,16 +221,21 @@
             for r in range(sub):
                 conv[r, pl.ds(pl.multiple_of(c0, 16), 16), :] = acc[r]
 
+        normed = norm(conv[...].reshape(sub * cols, width), gain1)
+        branch = jnp.zeros((sub * cols, width), F32)
+        units = mlp_in.shape[1]
+        for u in range(0, units, units // 2):
+            part = slice(u, u + units // 2)
+            h = jnp.dot(normed, mlp_in[:, part], preferred_element_type=F32)
+            inner = gelu(h).astype(BF16)
+            branch = branch + jnp.dot(inner, mlp_out[part, :], preferred_element_type=F32)
+        branch = (scale * branch).reshape(sub, cols, width)
         for r in range(sub):
-            normed = norm(conv[r], gain1)
-            h = jnp.dot(normed, mlp_in[...], preferred_element_type=F32)
-            inner = gelu(h).astype(BF16)
-            branch = jnp.dot(inner, mlp_out[...], preferred_element_type=F32)
-            mid[s, d, r] = (fields[0, first + r].astype(F32) + scale * branch).astype(BF16)
-
-        @pl.when(k < n - 1)
-        def _():
-            to_mixer(s, d).start()
+            mid[s, d, r] = (fields[0, first + r].astype(F32) + branch[r]).astype(BF16)
+
+            @pl.when(k < n - 1)
+            def _(r=r):
+                to_mixer(s, d, r).start()
 
         @pl.when(k == n - 1)
         def _():
@@ -216,38 +243,42 @@
 
     few = n <= 8
 
-    def each_member(body):
-        if few:
-            for m in range(n):
-                body(m)
-        else:
-            pl.loop(0, n)(body)
-
     def mix(s):
-        @pl.loop(0, n - 1)
-        def _(k):
-            from_member(s, other(k)).wait_recv()
-
         @pl.loop(0, sub)
         def _(r):
-            def project(m):
-                normed = norm(recv[s, m, r].astype(F32), gain2)
-                q_s[m] = jnp.dot(normed, qkv[0], preferred_element_type=F32).astype(BF16)
-                k_s[m] = jnp.dot(normed, qkv[1], preferred_element_type=F32).astype(BF16)
-                v_s[m] = jnp.dot(normed, qkv[2], preferred_element_type=F32).astype(BF16)
-
-            def attend(m):
-                def score(j):
-                    prod = q_s[m].astype(F32) * k_s[j].astype(F32)
-                    return jnp.dot(prod.astype(BF16), ones, preferred_element_type=F32)
+            @pl.loop(0, n - 1)
+            def _(k):
+                from_member(s, other(k), r).wait_recv()
+
+            def project(m, many):
+                x = recv[s, pl.ds(m, many), r].astype(F32).reshape(many * cols, width)
+                normed = norm(x, gain2)
+                got = jnp.dot(normed, qkv_s[...], preferred_element_type=F32)
+                got = got.reshape(many, cols, 3 * width)
+                q_s[pl.ds(m, many)] = got[:, :, 0:width].astype(BF16)
+                k_s[pl.ds(m, many)] = got[:, :, width : 2 * width].astype(BF16)
+                v_s[pl.ds(m, many)] = got[:, :, 2 * width :].astype(BF16).astype(F32)
+
+            def attend(k):
+                m = other(k)
+                query = q_s[m]
+
+                def score(*js):
+                    prod = jnp.concatenate([query * k_s[j] for j in js], axis=1)
+                    take = ones[: prod.shape[1], : prod.shape[1]]
+                    return jnp.dot(prod, take, preferred_element_type=F32)
 
                 if few:
-                    scores = [score(j) for j in range(n)]
+                    scores = []
+                    for j in range(0, n, 2):
+                        js = range(j, min(j + 2, n))
+                        pair = score(*js)
+                        scores += [pair[:, i * width : (i + 1) * width] for i in range(len(js))]
                     top = functools.reduce(jnp.maximum, scores)
                     den, acc = None, None
                     for j in range(n):
                         e = jnp.exp2((scores[j] - top) * factor)
-                        term = e * v_s[j].astype(F32)
+                        term = e * v_s[j]
                         den = e if den is None else den + e
                         acc = term if acc is None else acc + term
                 else:
@@ -257,34 +288,35 @@
                         now = jnp.maximum(top, sc)
                         keep = jnp.exp2((top - now) * factor)
                         e = jnp.exp2((sc - now) * factor)
-                        return now, den * keep + e, acc * keep + e * v_s[j].astype(F32)
+                        return now, den * keep + e, acc * keep + e * v_s[j]
 
                     _, den, acc = lax.fori_loop(
-                        1, n, more,
-                        (score(0), jnp.ones((cols, width), F32), v_s[0].astype(F32)),
+                        1, n, more, (score(0), jnp.ones((cols, width), F32), v_s[0])
                     )
                 mixed = (acc / den).astype(BF16)
                 proj = jnp.dot(mixed, out_weight[...], preferred_element_type=F32)
                 back[s, m, r] = (recv[s, m, r].astype(F32) + proj).astype(BF16)
 
-            each_member(project)
-            each_member(attend)
-
-        @pl.loop(0, n - 1)
-        def _(k):
-            to_member(s, other(k)).start()
+                @pl.when(k < n - 1)
+                def _():
+                    to_member(s, m, r).start()
+
+            if few:
+                project(0, n)
+                for k in range(n):
+                    attend(k)
+            else:
+                pl.loop(0, n)(lambda m: project(m, 1))
+                pl.loop(0, n)(attend)
 
         out[0, pl.ds(me * share + s * sub, sub)] = back[s, me]
 
-    @pl.loop(0, steps + 1)
-    def _(s):
-        @pl.when(s < steps)
-        def _():
-            pl.loop(0, n)(lambda k: block(s, k))
-
-        @pl.when(s >= 1)
-        def _():
-            mix(s - 1)
+    for low, high in ((0, half), (half, n)):
+        @pl.loop(0, steps)
+        def _(s, low=low, high=high):
+            pl.loop(low, high)(lambda k: block(s, k))
+
+    pl.loop(0, steps)(mix)
 
     for a, b in SIDES:
         @pl.when(exists(a, b))
@@ -296,9 +328,12 @@
         @pl.loop(0, n - 1)
         def _(k):
             d = other(k)
-            to_mixer(s, d).wait_send()
-            to_member(s, d).wait_send()
-            from_mixer(s, d).wait_recv()
+
+            @pl.loop(0, sub)
+            def _(r):
+                to_mixer(s, d, r).wait_send()
+                to_member(s, d, r).wait_send()
+                from_mixer(s, d, r).wait_recv()
 
 
 SUB = 4
@@ -316,9 +351,11 @@
     return pl.pallas_call(
         functools.partial(kernel, n, row_n, col_n, sub),
         out_shape=jax.ShapeDtypeStruct(fields.shape, fields.dtype),
-        in_specs=[vmem] * len(args),
+        in_specs=[pl.BlockSpec(memory_space=pl.ANY)] * len(args),
         out_specs=vmem,
-        scratch_shapes=[
+        scratch_shapes=[pltpu.VMEM(x.shape, x.dtype) for x in args[1:]] + [
+            pltpu.VMEM(fields.shape, fields.dtype),
+            dma((len(args),)),
             pltpu.VMEM((rows + 2 * HALO, cols + 2 * PAD, width), F32),
             pltpu.VMEM((KERNEL, 8, width), F32),
             pltpu.VMEM((sub, cols, width), F32),
@@ -327,19 +364,20 @@
             pltpu.VMEM(blocks, BF16),
             pltpu.VMEM((n, cols, width), BF16),
             pltpu.VMEM((n, cols, width), BF16),
-            pltpu.VMEM((n, cols, width), BF16),
+            pltpu.VMEM((n, cols, width), F32),
+            pltpu.VMEM((width, 3 * width), BF16),
             pltpu.VMEM((2, HALO, cols, width), BF16),
             pltpu.VMEM((2, rows, PAD, width), BF16),
             pltpu.VMEM((4, HALO, PAD, width), BF16),
             dma((8,)),
             dma((8,)),
-            dma((steps, n)),
-            dma((steps, n)),
-            dma((steps, n)),
-            dma((steps, n)),
+            dma((steps, n, sub)),
+            dma((steps, n, sub)),
+            dma((steps, n, sub)),
+            dma((steps, n, sub)),
         ],
         compiler_params=pltpu.CompilerParams(
-            collective_id=0, has_side_effects=True, vmem_limit_bytes=48 * 1024 * 1024
+            collective_id=0, has_side_effects=True, vmem_limit_bytes=56 * 1024 * 1024
         ),
     )(*args)
 

time: 66.4 us -> 62.8 us (0.946); the launches traced: 65.4 us -> 62.6 us
  local copies, waits for them, and re-layouts: 8.33 us -> 2.31 us
  Pallas kernels: 57 us -> 60.3 us
    unnamed x19 -> x1, local copies, waits for them, and re-layouts: 8.33 us -> 2.31 us
    pallas_call x1, Pallas kernels: 57 us -> 60.3 us  [shards(): pl.pallas_call(functools.partial(kernel, n, row_n, col_n, sub), out_shape...]
where the time goes in v2:
time: 62.8 us; the launch traced here: 62.6 us
  Pallas kernels  60.3 us (96%)
  local copies, waits for them, and re-layouts  2.31 us (4%)
    pallas_call x1, Pallas kernels, shards(): pl.pallas_call(functools.partial(kernel, n, row_n, col_n, sub), out_shape...  60.3 us
    unnamed x1, local copies, waits for them, and re-layouts  2.31 us

profile of v2, /device:TPU:0, one launch (start us, length us, event | category | flops | bytes accessed | tf_op | source)
XLA Modules:
  0.0 62.6 jit_solution(17834642842083368223)
XLA Ops:
  0.0 60.3 %shard_map.91 = bf16[1,32,128,128]{3,2,1,0:T(8,128)(2,1)} custom-call(bf16[1,32,128,128]{3,2,1,0:T(8,128)(2,1)} %fields_hbm.1, bf16[7,7,128]{2,1,0:T(8,128)(2,1)} %refs_0_.1, bf16[128]{0:T(256)(128)(2,1)} %refs_1_.1, bf16[128,512]{1,0:T(8,128)(2,1)} %refs_2_.1, bf16[512,128]{1,0:T(8,128)(2,1)} %refs_3_.1, bf16[128]{0:T(256)(128)(2,1)} %refs_4_.1, ...), custom_call_target="tpu_custom_call" | custom-call | tf_op jit(solution)/shard_map/pallas_call | solution.py:351
  60.3 2.3 %copy.11 = bf16[1,32,128,128]{3,2,1,0:T(8,128)(2,1)} copy(bf16[1,32,128,128]{3,2,1,0:T(8,128)(2,1)} %shard_map.91) | data formatting | bytes 2097152

commit v3 on v2

--- a/solution.py
+++ b/solution.py
@@ -70,7 +70,7 @@
         if n % 2:
             return lax.rem(me + 1 + k, n)
         side = me // half
-        far = (1 - side) * half + lax.rem(me + k, half)
+        far = jnp.where(side == 0, half + k, half - 1 - k)
         near = side * half + lax.rem(me + 1 + k, half)
         return jnp.where(k < half, far, near)
 
@@ -132,25 +132,29 @@
             slice(0, PAD) if b < 0 else slice(PAD + cols, 2 * PAD + cols))
         return r, c
 
-    for a, b in SIDES:
-        here = exists(a, b)
-        r, c = spot(a, b)
-
-        @pl.when(here)
-        def _(a=a, b=b, r=r, c=c):
-            pltpu.make_async_remote_copy(
-                src_ref=halo_ref(a, b),
-                dst_ref=halo_ref(a, b),
-                send_sem=halo_send.at[SIDES.index((a, b))],
-                recv_sem=halo_recv.at[SIDES.index((a, b))],
-                device_id={"row": row_i + a, "col": col_i + b},
-                device_id_type=MESH,
-            ).wait_recv()
-            pad[r, c, :] = halo_ref(a, b)[...].astype(F32)
-
-        @pl.when(jnp.logical_not(here))
-        def _(r=r, c=c):
-            pad[r, c, :] = jnp.zeros((r.stop - r.start, c.stop - c.start, width), F32)
+    def take(sides):
+        for a, b in sides:
+            here = exists(a, b)
+            r, c = spot(a, b)
+
+            @pl.when(here)
+            def _(a=a, b=b, r=r, c=c):
+                pltpu.make_async_remote_copy(
+                    src_ref=halo_ref(a, b),
+                    dst_ref=halo_ref(a, b),
+                    send_sem=halo_send.at[SIDES.index((a, b))],
+                    recv_sem=halo_recv.at[SIDES.index((a, b))],
+                    device_id={"row": row_i + a, "col": col_i + b},
+                    device_id_type=MESH,
+                ).wait_recv()
+                pad[r, c, :] = halo_ref(a, b)[...].astype(F32)
+
+            @pl.when(jnp.logical_not(here))
+            def _(r=r, c=c):
+                pad[r, c, :] = jnp.zeros((r.stop - r.start, c.stop - c.start, width), F32)
+
+    late = sub >= HALO
+    take([side for side in SIDES if side[0] == 0 or not late])
 
     gain1 = conv_gain[...].astype(F32).reshape(1, width)
     gain2 = attn_gain[...].astype(F32).reshape(1, width)
@@ -205,6 +209,9 @@
     def block(s, k):
         d = other(k)
         first = d * share + s * sub
+        if late:
+            for a, edge in ((-1, 0), (1, rows - sub)):
+                pl.when(first == edge)(lambda a=a: take([side for side in SIDES if side[0] == a]))
 
         @pl.loop(0, cols // 16)
         def _(j):
@@ -351,7 +358,7 @@
     return pl.pallas_call(
         functools.partial(kernel, n, row_n, col_n, sub),
         out_shape=jax.ShapeDtypeStruct(fields.shape, fields.dtype),
-        in_specs=[pl.BlockSpec(memory_space=pl.ANY)] * len(args),
+        in_specs=[pl.BlockSpec(memory_space=pltpu.HBM)] * len(args),
         out_specs=vmem,
         scratch_shapes=[pltpu.VMEM(x.shape, x.dtype) for x in args[1:]] + [
             pltpu.VMEM(fields.shape, fields.dtype),

time: 62.8 us -> 60.3 us (0.960)
  Pallas kernels: 60.3 us -> 57.9 us
    pallas_call x1, Pallas kernels: 60.3 us -> 57.9 us  [shards(): pl.pallas_call(functools.partial(kernel, n, row_n, col_n, sub), out_shape...]
where the time goes in v3:
time: 60.3 us; the launch traced here: 60.2 us
  Pallas kernels  57.9 us (96%)
  local copies, waits for them, and re-layouts  2.31 us (4%)
    pallas_call x1, Pallas kernels, shards(): pl.pallas_call(functools.partial(kernel, n, row_n, col_n, sub), out_shape...  57.9 us
    unnamed x1, local copies, waits for them, and re-layouts  2.31 us

profile of v3, /device:TPU:0, one launch (start us, length us, event | category | flops | bytes accessed | tf_op | source)
XLA Modules:
  0.0 60.2 jit_solution(7717344323053298001)
XLA Ops:
  0.0 57.9 %shard_map.91 = bf16[1,32,128,128]{3,2,1,0:T(8,128)(2,1)} custom-call(bf16[1,32,128,128]{3,2,1,0:T(8,128)(2,1)} %fields_hbm.1, bf16[7,7,128]{2,1,0:T(8,128)(2,1)} %refs_0_.1, bf16[128]{0:T(256)(128)(2,1)} %refs_1_.1, bf16[128,512]{1,0:T(8,128)(2,1)} %refs_2_.1, bf16[512,128]{1,0:T(8,128)(2,1)} %refs_3_.1, bf16[128]{0:T(256)(128)(2,1)} %refs_4_.1, ...), custom_call_target="tpu_custom_call" | custom-call | tf_op jit(solution)/shard_map/pallas_call | solution.py:358
  57.9 2.3 %copy.11 = bf16[1,32,128,128]{3,2,1,0:T(8,128)(2,1)} copy(bf16[1,32,128,128]{3,2,1,0:T(8,128)(2,1)} %shard_map.91) | data formatting | bytes 2097152

commit v4 on v3

--- a/solution.py
+++ b/solution.py
@@ -12,6 +12,7 @@
 KERNEL = 7
 HALO = KERNEL // 2
 PAD = 16
+PIECES = 2
 MESH = pl.DeviceIdType.MESH
 F32 = jnp.float32
 BF16 = jnp.bfloat16
@@ -44,6 +45,7 @@
     _, rows, cols, width = fields.shape
     share = rows // n
     steps = share // sub
+    piece = cols // PIECES
     me = lax.axis_index("ens")
     row_i = lax.axis_index("row")
     col_i = lax.axis_index("col")
@@ -189,7 +191,7 @@
     def to_member(s, d, r):
         return pltpu.make_async_remote_copy(
             src_ref=back.at[s, d, r],
-            dst_ref=out.at[0, me * share + s * sub + r],
+            dst_ref=out.at[0, pl.ds(me * share + s * sub, sub), pl.ds(pl.multiple_of(r * piece, 16), piece)],
             send_sem=send2.at[s, d, r],
             recv_sem=recv2.at[s, me, r],
             device_id={"ens": d},
@@ -199,7 +201,7 @@
     def from_mixer(s, d, r):
         return pltpu.make_async_remote_copy(
             src_ref=back.at[s, d, r],
-            dst_ref=out.at[0, d * share + s * sub + r],
+            dst_ref=out.at[0, pl.ds(d * share + s * sub, sub), pl.ds(pl.multiple_of(r * piece, 16), piece)],
             send_sem=send2.at[s, d, r],
             recv_sem=recv2.at[s, d, r],
             device_id={"ens": d},
@@ -213,36 +215,40 @@
             for a, edge in ((-1, 0), (1, rows - sub)):
                 pl.when(first == edge)(lambda a=a: take([side for side in SIDES if side[0] == a]))
 
-        @pl.loop(0, cols // 16)
-        def _(j):
-            c0 = j * 16
-            acc = [jnp.zeros((16, width), F32) for _ in range(sub)]
-            for b in range(KERNEL):
-                lines = [
-                    pad[first + r, pl.ds(c0 + (PAD - HALO + b), 16), :]
-                    for r in range(sub + KERNEL - 1)
-                ]
-                for a in range(KERNEL):
-                    w = taps[a, b : b + 1, :]
-                    acc = [acc[r] + lines[r + a] * w for r in range(sub)]
-            for r in range(sub):
-                conv[r, pl.ds(pl.multiple_of(c0, 16), 16), :] = acc[r]
-
-        normed = norm(conv[...].reshape(sub * cols, width), gain1)
-        branch = jnp.zeros((sub * cols, width), F32)
-        units = mlp_in.shape[1]
-        for u in range(0, units, units // 2):
-            part = slice(u, u + units // 2)
-            h = jnp.dot(normed, mlp_in[:, part], preferred_element_type=F32)
-            inner = gelu(h).astype(BF16)
-            branch = branch + jnp.dot(inner, mlp_out[part, :], preferred_element_type=F32)
-        branch = (scale * branch).reshape(sub, cols, width)
-        for r in range(sub):
-            mid[s, d, r] = (fields[0, first + r].astype(F32) + branch[r]).astype(BF16)
+        @pl.loop(0, PIECES)
+        def _(p):
+            start = pl.multiple_of(p * piece, 16)
+
+            @pl.loop(0, piece // 16)
+            def _(j):
+                c0 = start + j * 16
+                acc = [jnp.zeros((16, width), F32) for _ in range(sub)]
+                for b in range(KERNEL):
+                    lines = [
+                        pad[first + r, pl.ds(c0 + (PAD - HALO + b), 16), :]
+                        for r in range(sub + KERNEL - 1)
+                    ]
+                    for a in range(KERNEL):
+                        w = taps[a, b : b + 1, :]
+                        acc = [acc[r] + lines[r + a] * w for r in range(sub)]
+                for r in range(sub):
+                    conv[r, pl.ds(pl.multiple_of(j * 16, 16), 16), :] = acc[r]
+
+            normed = norm(conv[...].reshape(sub * piece, width), gain1)
+            branch = jnp.zeros((sub * piece, width), F32)
+            units = mlp_in.shape[1]
+            for u in range(0, units, units // 2):
+                part = slice(u, u + units // 2)
+                h = jnp.dot(normed, mlp_in[:, part], preferred_element_type=F32)
+                inner = gelu(h).astype(BF16)
+                branch = branch + jnp.dot(inner, mlp_out[part, :], preferred_element_type=F32)
+            branch = (scale * branch).reshape(sub, piece, width)
+            kept = fields[0, pl.ds(first, sub), pl.ds(start, piece), :].astype(F32)
+            mid[s, d, p] = (kept + branch).astype(BF16)
 
             @pl.when(k < n - 1)
-            def _(r=r):
-                to_mixer(s, d, r).start()
+            def _():
+                to_mixer(s, d, p).start()
 
         @pl.when(k == n - 1)
         def _():
@@ -251,17 +257,17 @@
     few = n <= 8
 
     def mix(s):
-        @pl.loop(0, sub)
+        @pl.loop(0, PIECES)
         def _(r):
             @pl.loop(0, n - 1)
             def _(k):
                 from_member(s, other(k), r).wait_recv()
 
             def project(m, many):
-                x = recv[s, pl.ds(m, many), r].astype(F32).reshape(many * cols, width)
+                x = recv[s, pl.ds(m, many), r].astype(F32).reshape(many * sub * piece, width)
                 normed = norm(x, gain2)
                 got = jnp.dot(normed, qkv_s[...], preferred_element_type=F32)
-                got = got.reshape(many, cols, 3 * width)
+                got = got.reshape(many, sub * piece, 3 * width)
                 q_s[pl.ds(m, many)] = got[:, :, 0:width].astype(BF16)
                 k_s[pl.ds(m, many)] = got[:, :, width : 2 * width].astype(BF16)
                 v_s[pl.ds(m, many)] = got[:, :, 2 * width :].astype(BF16).astype(F32)
@@ -298,11 +304,11 @@
                         return now, den * keep + e, acc * keep + e * v_s[j]
 
                     _, den, acc = lax.fori_loop(
-                        1, n, more, (score(0), jnp.ones((cols, width), F32), v_s[0])
+                        1, n, more, (score(0), jnp.ones((sub * piece, width), F32), v_s[0])
                     )
                 mixed = (acc / den).astype(BF16)
                 proj = jnp.dot(mixed, out_weight[...], preferred_element_type=F32)
-                back[s, m, r] = (recv[s, m, r].astype(F32) + proj).astype(BF16)
+                back[s, m, r] = (recv[s, m, r].astype(F32) + proj.reshape(sub, piece, width)).astype(BF16)
 
                 @pl.when(k < n - 1)
                 def _():
@@ -316,7 +322,9 @@
                 pl.loop(0, n)(lambda m: project(m, 1))
                 pl.loop(0, n)(attend)
 
-        out[0, pl.ds(me * share + s * sub, sub)] = back[s, me]
+        for p in range(PIECES):
+            rows_here = pl.ds(me * share + s * sub, sub)
+            out[0, rows_here, p * piece : (p + 1) * piece, :] = back[s, me, p]
 
     for low, high in ((0, half), (half, n)):
         @pl.loop(0, steps)
@@ -336,7 +344,7 @@
         def _(k):
             d = other(k)
 
-            @pl.loop(0, sub)
+            @pl.loop(0, PIECES)
             def _(r):
                 to_mixer(s, d, r).wait_send()
                 to_member(s, d, r).wait_send()
@@ -354,7 +362,8 @@
     steps = share // sub
     vmem = pl.BlockSpec(memory_space=pltpu.VMEM)
     dma = pltpu.SemaphoreType.DMA
-    blocks = (steps, n, sub, cols, width)
+    piece = cols // PIECES
+    blocks = (steps, n, PIECES, sub, piece, width)
     return pl.pallas_call(
         functools.partial(kernel, n, row_n, col_n, sub),
         out_shape=jax.ShapeDtypeStruct(fields.shape, fields.dtype),
@@ -365,23 +374,23 @@
             dma((len(args),)),
             pltpu.VMEM((rows + 2 * HALO, cols + 2 * PAD, width), F32),
             pltpu.VMEM((KERNEL, 8, width), F32),
-            pltpu.VMEM((sub, cols, width), F32),
+            pltpu.VMEM((sub, piece, width), F32),
             pltpu.VMEM(blocks, BF16),
             pltpu.VMEM(blocks, BF16),
             pltpu.VMEM(blocks, BF16),
-            pltpu.VMEM((n, cols, width), BF16),
-            pltpu.VMEM((n, cols, width), BF16),
-            pltpu.VMEM((n, cols, width), F32),
+            pltpu.VMEM((n, sub * piece, width), BF16),
+            pltpu.VMEM((n, sub * piece, width), BF16),
+            pltpu.VMEM((n, sub * piece, width), F32),
             pltpu.VMEM((width, 3 * width), BF16),
             pltpu.VMEM((2, HALO, cols, width), BF16),
             pltpu.VMEM((2, rows, PAD, width), BF16),
             pltpu.VMEM((4, HALO, PAD, width), BF16),
             dma((8,)),
             dma((8,)),
-            dma((steps, n, sub)),
-            dma((steps, n, sub)),
-            dma((steps, n, sub)),
-            dma((steps, n, sub)),
+            dma((steps, n, PIECES)),
+            dma((steps, n, PIECES)),
+            dma((steps, n, PIECES)),
+            dma((steps, n, PIECES)),
         ],
         compiler_params=pltpu.CompilerParams(
             collective_id=0, has_side_effects=True, vmem_limit_bytes=56 * 1024 * 1024

time: 60.3 us -> 58.9 us (0.977)
  Pallas kernels: 57.9 us -> 56.5 us
    pallas_call x1, Pallas kernels: 57.9 us -> 56.5 us  [shards(): pl.pallas_call(functools.partial(kernel, n, row_n, col_n, sub), out_shape...]
where the time goes in v4:
time: 58.9 us; the launch traced here: 58.8 us
  Pallas kernels  56.5 us (96%)
  local copies, waits for them, and re-layouts  2.31 us (4%)
    pallas_call x1, Pallas kernels, shards(): pl.pallas_call(functools.partial(kernel, n, row_n, col_n, sub), out_shape...  56.5 us
    unnamed x1, local copies, waits for them, and re-layouts  2.31 us

profile of v4, /device:TPU:0, one launch (start us, length us, event | category | flops | bytes accessed | tf_op | source)
XLA Modules:
  0.0 58.8 jit_solution(10866436025359736211)
XLA Ops:
  0.0 56.5 %shard_map.91 = bf16[1,32,128,128]{3,2,1,0:T(8,128)(2,1)} custom-call(bf16[1,32,128,128]{3,2,1,0:T(8,128)(2,1)} %fields_hbm.1, bf16[7,7,128]{2,1,0:T(8,128)(2,1)} %refs_0_.1, bf16[128]{0:T(256)(128)(2,1)} %refs_1_.1, bf16[128,512]{1,0:T(8,128)(2,1)} %refs_2_.1, bf16[512,128]{1,0:T(8,128)(2,1)} %refs_3_.1, bf16[128]{0:T(256)(128)(2,1)} %refs_4_.1, ...), custom_call_target="tpu_custom_call" | custom-call | tf_op jit(solution)/shard_map/pallas_call | solution.py:367
  56.5 2.3 %copy.11 = bf16[1,32,128,128]{3,2,1,0:T(8,128)(2,1)} copy(bf16[1,32,128,128]{3,2,1,0:T(8,128)(2,1)} %shard_map.91) | data formatting | bytes 2097152
